TPU v7x, 256 devices: a whole 4x4x8 slice. The times are simulated.
256 devices in a mesh: dp: 32 (over x, y, core), vocab: 8 (over z).
Axes of the slice: x: 4, y: 4, z: 8, core: 2. Of those that a mesh axis runs over, the one named last changes fastest.
Arguments:
- encoder_proj: bfloat16 [6144, 512], P('dp'), may hold values from -4 to 4
- predictor_proj: bfloat16 [128, 64, 512], P('dp'), may hold values from -5 to 5
- out_weight: bfloat16 [512, 30720], P(None, 'vocab'), may hold values from -1 to 1
- frame_utt: int32 [6144], P('dp'), may hold values from 0 to 127, as said below
- prune_start: int32 [6144], P('dp'), may hold values from 0 to 59, as said below
- labels: int32 [6144, 5], P('dp'), may hold values from 1 to 30719
- utt_len: int32 [128], replicated, may hold values from 5 to 63
- blank_occ: float32 [6144, 5], P('dp'), may hold values from 0.05 to 1
- label_occ: float32 [6144, 5], P('dp'), may hold values from 0.05 to 1
- frame_weight: float32 [6144], P('dp'), may hold values from 0.25 to 1
Outputs:
- grad_weight: float32 [512, 30720], P('dp', 'vocab')
- grad_encoder: float32 [6144, 512], P('dp', 'vocab')
- grad_predictor: float32 [128, 64, 512], P('dp', None, 'vocab')
Inputs may be any that keep to these rules, and one draw needn't show every extreme that they name: `frame_utt`: frames are in utterance order; the utterances of index d of dp are d * 4 to (d + 1) * 4 - 1, and each frame belongs to an utterance of its own index of dp or of the index before. prune_start[t] + 4 is at most utt_len[frame_utt[t]].
All inputs are finite; a program needn't handle non-finite values.
Results may differ from a plain program's by a relative error of at most 0.0043.
Values may be sent and summed in bfloat16 or wider, within the bound.
A program may use at most 64 MiB of HBM per device.

v0:
```python
import jax
import jax.numpy as jnp
from jax import lax
from jax.sharding import PartitionSpec as P


def passed_along(value, axis, steps):
    count = lax.axis_size(axis)
    first, last = (max(0, -steps), min(count, count - steps))
    return lax.ppermute(value, axis, [(source, source + steps) for source in range(first, last)])


def body(
    encoder_proj,
    predictor_proj,
    out_weight,
    frame_utt,
    prune_start,
    labels,
    utt_len,
    blank_occ,
    label_occ,
    frame_weight,
):
    frame_count, kept = labels.shape
    slots, depth, width = predictor_proj.shape
    vocab_local = out_weight.shape[1]
    row_count = frame_count * kept
    table_rows = 2 * slots * depth
    here = lax.axis_index("dp")
    earlier = passed_along(predictor_proj, "dp", 1)
    table = jnp.concatenate([earlier, predictor_proj], axis=0).reshape(table_rows, width)
    offsets = jnp.arange(kept, dtype=jnp.int32)
    positions = prune_start[:, None] + offsets[None, :]
    slot_local = frame_utt - (here - 1) * slots
    row_index = (slot_local[:, None] * depth + positions).reshape(row_count)
    picker_bool = row_index[:, None] == jnp.arange(table_rows, dtype=jnp.int32)[None, :]
    picked = jnp.dot(picker_bool.astype(jnp.bfloat16), table, preferred_element_type=jnp.float32)
    lookup = frame_utt[:, None] == jnp.arange(utt_len.shape[0], dtype=jnp.int32)[None, :]
    limits = jnp.sum(jnp.where(lookup, utt_len[None, :], 0), axis=1)
    validity = (positions < limits[:, None]).astype(jnp.float32)
    blank_coef = (frame_weight[:, None] * blank_occ).reshape(row_count, 1)
    label_coef = (frame_weight[:, None] * label_occ * validity).reshape(row_count, 1)
    summed = jnp.repeat(encoder_proj, kept, axis=0).astype(jnp.float32) + picked
    joint_act = jnp.tanh(summed)
    joint_low = joint_act.astype(jnp.bfloat16)
    logits = jnp.dot(joint_low, out_weight, preferred_element_type=jnp.float32)
    peak = lax.pmax(jnp.max(logits, axis=1), "vocab")
    expon = jnp.exp(logits - peak[:, None])
    total = lax.psum(jnp.sum(expon, axis=1), "vocab")
    columns = lax.axis_index("vocab") * vocab_local + jnp.arange(vocab_local, dtype=jnp.int32)
    ids_flat = labels.reshape(row_count, 1)
    is_blank = (columns[None, :] == 0).astype(jnp.float32)
    is_label = (columns[None, :] == ids_flat).astype(jnp.float32)
    logit_grad = (
        (blank_coef + label_coef) * (expon / total[:, None])
        - blank_coef * is_blank
        - label_coef * is_label
    )
    grad_low = logit_grad.astype(jnp.bfloat16)
    partial_hidden = lax.dot_general(
        grad_low, out_weight, (((1,), (1,)), ((), ())), preferred_element_type=jnp.float32
    )
    share_width = width // lax.axis_size("vocab")
    share_start = lax.axis_index("vocab") * share_width
    hidden_part = lax.psum_scatter(partial_hidden, "vocab", scatter_dimension=1, tiled=True)
    act_part = lax.dynamic_slice_in_dim(joint_act, share_start, share_width, 1)
    act_grad = hidden_part * (1.0 - act_part * act_part)
    grad_encoder = jnp.sum(act_grad.reshape(frame_count, kept, share_width), axis=1)
    picker_wide = picker_bool.astype(jnp.float32)
    slot_grads = lax.dot_general(
        picker_wide,
        act_grad,
        (((0,), (0,)), ((), ())),
        precision=lax.Precision.HIGHEST,
        preferred_element_type=jnp.float32,
    )
    slot_grads = slot_grads.reshape(2 * slots, depth, share_width)
    returned = passed_along(slot_grads[:slots], "dp", -1)
    grad_predictor = slot_grads[slots:] + returned
    weight_term = lax.dot_general(
        joint_low, grad_low, (((0,), (0,)), ((), ())), preferred_element_type=jnp.float32
    )
    grad_weight = lax.psum_scatter(weight_term, "dp", scatter_dimension=0, tiled=True)
    return (grad_weight, grad_encoder, grad_predictor)


def solution(mesh):
    in_specs = (
        P("dp", None),
        P("dp", None, None),
        P(None, "vocab"),
        P("dp"),
        P("dp"),
        P("dp", None),
        P(),
        P("dp", None),
        P("dp", None),
        P("dp"),
    )
    out_specs = (P("dp", "vocab"), P("dp", "vocab"), P("dp", None, "vocab"))
    return jax.shard_map(body, mesh=mesh, in_specs=in_specs, out_specs=out_specs, check_vma=False)
```

profile of v0, /device:TPU:1, one launch (start us, length us, event | category | flops | bytes accessed | tf_op | source)
XLA Modules:
  0.0 238.1 jit_solution(805398523559423015)
XLA Ops:
  7.2 0.0 copy-start.1
  7.2 0.0 reduce-scatter.7.cloned.1.call-start
  7.2 4.7 %collective-permute-start = (bf16[4,64,512]{2,1,0:T(8,128)(2,1)}, bf16[4,64,512]{2,1,0:T(8,128)(2,1)}, u32[]{:S(2)}, u32[]{:S(2)}) collective-permute-start(bf16[4,64,512]{2,1,0:T(8,128)(2,1)} %param.11), channel_id=1, source_target_pairs={{0,8},{8,16},{16,24},{24,32},{32,40},{40,48},{48,56},{56,64},{64,7... | collective-permute-start | bytes 786440 | tf_op jit(solution)/shard_map/ppermute | solution.py:10
  12.0 0.7 subtract_multiply_fusion.1
  12.6 0.9 select_reduce_fusion
  13.5 0.7 broadcast_multiply_fusion
  14.3 0.7 fusion.10
  15.0 0.1 copy.32
  15.1 0.2 reshape.81
  15.3 0.1 copy.31
  15.4 0.2 add.75
  15.6 0.1 copy.33
  15.7 0.2 reshape.82
  16.0 0.8 copy.34
  16.8 0.2 eq.61
  17.0 1.3 broadcast_in_dim.10
  18.3 1.5 convert_element_type.26
  19.8 0.0 collective-permute-done
  19.8 0.0 copy-done.1
  19.8 1.0 pad_maximum_fusion
  20.8 2.3 add_tanh_fusion
  23.1 9.6 %fusion.12 = (f32[960]{0:T(1024)S(1)}, f32[960,3840]{1,0:T(8,128)}) fusion(bf16[512,3840]{1,0:T(8,128)(2,1)} %param.12, f32[960,512]{1,0:T(8,128)S(1)} %add_tanh_fusion), kind=kOutput, calls=%fused_computation.27 | convolution fusion | flops 3779050496 | bytes 20647680 | tf_op jit(solution)/shard_map/dot_general | solution.py:47
  32.8 16.3 %pmax.7 = f32[960]{0:T(1024)S(1)} all-reduce(f32[960]{0:T(1024)S(1)} %get-tuple-element.13), channel_id=1, replica_groups=mesh['dp'=32,'vocab'=8] {'vocab'}, use_global_device_ids=true, to_apply=%region_2.3 | all-reduce | flops 960 | bytes 7680 | tf_op jit(solution)/shard_map/pmax | solution.py:48
  49.1 7.3 %fusion = f32[960]{0:T(1024)S(1)} fusion(f32[960,3840]{1,0:T(8,128)} %get-tuple-element.14, f32[960]{0:T(1024)S(1)} %pmax.7), kind=kLoop, calls=%fused_computation.2 | loop fusion | flops 7371840 | bytes 14753280 | tf_op jit(solution)/shard_map/reduce_sum | solution.py:50
  56.3 10.7 %psum.7 = f32[960]{0:T(1024)S(1)} all-reduce(f32[960]{0:T(1024)S(1)} %fusion), channel_id=1, replica_groups=mesh['dp'=32,'vocab'=8] {'vocab'}, use_global_device_ids=true, to_apply=%region_4.5 | all-reduce | flops 960 | bytes 7680 | tf_op jit(solution)/shard_map/psum | solution.py:50
  67.0 0.0 copy-start.2
  67.0 9.6 %subtract_convert_fusion = bf16[960,3840]{1,0:T(8,128)(2,1)S(1)} fusion(f32[960,3840]{1,0:T(8,128)} %get-tuple-element.14, f32[960]{0:T(1024)S(1)} %reshape.82, s32[3840]{0:T(1024)S(1)} %iota_add_fusion, f32[3840]{0:T(1024)S(1)} %compare_convert_fusion, f32[960]{0:T(1024)S(1)} %reshape.81, f32[960]{0:T(1024)S(1)} %psum.7, f32[960]{0:T(1024)S(1)} %pmax.7, ...), kind=kLoop, calls=%fused_computation | loop fusion | flops 33177600 | bytes 22172160 | tf_op jit(solution)/shard_map/convert_element_type | solution.py:60
  76.6 0.0 copy-start
  76.6 3.0 %copy-done = bf16[960,3840]{1,0:T(8,128)(2,1)} copy-done((bf16[960,3840]{1,0:T(8,128)(2,1)}, bf16[960,3840]{1,0:T(8,128)(2,1)S(1)}, u32[]{:S(2)}) %copy-start) | copy-done | bytes 7372824
  79.6 0.0 copy-done.2
  79.6 5.6 %convolution_bitcast_fusion = f32[512,960]{1,0:T(8,128)} fusion(bf16[960,3840]{1,0:T(8,128)(2,1)S(1)} %subtract_convert_fusion, bf16[512,3840]{1,0:T(8,128)(2,1)S(1)} %copy-done.2), kind=kOutput, calls=%fused_computation.7 | convolution fusion | flops 3774873600 | bytes 13271040
  85.2 0.0 reduce-scatter.7.cloned.1.call-update
  85.2 0.2 reduce-scatter.5.cloned.1.call-start
  85.4 9.5 %fusion.5 = f32[512,3840]{1,0:T(8,128)} fusion(bf16[960,3840]{1,0:T(8,128)(2,1)} %copy-done, f32[960,512]{1,0:T(8,128)S(1)} %add_tanh_fusion), kind=kOutput, calls=%fused_computation.12 | convolution fusion | flops 3775365120 | bytes 17203200 | tf_op jit(solution)/shard_map/dot_general | solution.py:81
  95.0 0.0 reduce-scatter.5.cloned.1.call-update
  95.0 32.6 %reduce-scatter.7.cloned.1.call-done = f32[64,960]{1,0:T(8,128)} async-done(((f32[512,960]{1,0:T(8,128)}), f32[64,960]{1,0:T(8,128)}) %reduce-scatter.7.cloned.1.call-update) | async-done | bytes 245776
  127.6 1.1 copy.43
  128.8 0.2 subtract_multiply_fusion
  129.0 0.9 fusion.1
  129.9 0.1 copy.41
  130.0 6.6 %collective-permute-start.1 = (f32[4,64,64]{2,1,0:T(8,128)S(1)}, f32[4,64,64]{2,1,0:T(8,128)S(1)}, u32[]{:S(2)}, u32[]{:S(2)}) collective-permute-start(f32[4,64,64]{2,1,0:T(8,128)S(1)} %bitcast.15), channel_id=1, source_target_pairs={{8,0},{16,8},{24,16},{32,24},{40,32},{48,40},{56,48},{64,56},{72,6... | collective-permute-start | bytes 196616 | tf_op jit(solution)/shard_map/ppermute | solution.py:10
  136.6 0.1 reshape.83
  136.7 0.1 copy.40
  136.8 0.2 reduce_sum.29
  137.0 0.7 copy.38
  137.8 2.7 %collective-permute-done.1 = f32[4,64,64]{2,1,0:T(8,128)S(1)} collective-permute-done((f32[4,64,64]{2,1,0:T(8,128)S(1)}, f32[4,64,64]{2,1,0:T(8,128)S(1)}, u32[]{:S(2)}, u32[]{:S(2)}) %collective-permute-start.1) | collective-permute-done | bytes 65568 | tf_op jit(solution)/shard_map/ppermute | solution.py:10
  140.4 0.7 add.81
  141.1 90.1 %reduce-scatter.5.cloned.1.call-done = f32[16,3840]{1,0:T(8,128)} async-done(((f32[512,3840]{1,0:T(8,128)}), f32[16,3840]{1,0:T(8,128)}) %reduce-scatter.5.cloned.1.call-update) | async-done | bytes 245776 | tf_op jit(solution)/shard_map/reduce_scatter | solution.py:84
  (4 shorter events, 0.0 us)
Async XLA Ops:
  7.2 12.7 %copy-start.1 = (bf16[4,64,512]{2,1,0:T(8,128)(2,1)S(1)}, bf16[4,64,512]{2,1,0:T(8,128)(2,1)}, u32[]{:S(2)}) copy-start(bf16[4,64,512]{2,1,0:T(8,128)(2,1)} %param.11) | copy-start | bytes 786436
  7.2 120.5 %reduce-scatter.7.cloned.1.call-start = ((), (), s32[]{:S(2)}) async-start(), calls=%async_computation.3 | async-start | bytes 2359296
  7.2 12.6 %collective-permute-start = (bf16[4,64,512]{2,1,0:T(8,128)(2,1)}, bf16[4,64,512]{2,1,0:T(8,128)(2,1)}, u32[]{:S(2)}, u32[]{:S(2)}) collective-permute-start(bf16[4,64,512]{2,1,0:T(8,128)(2,1)} %param.11), channel_id=1, source_target_pairs={{0,8},{8,16},{16,24},{24,32},{32,40},{40,48},{48,56},{56,64},{64,7... | collective-permute-start | bytes 786440 | tf_op jit(solution)/shard_map/ppermute | solution.py:10
  67.0 12.6 %copy-start.2 = (bf16[512,3840]{1,0:T(8,128)(2,1)S(1)}, bf16[512,3840]{1,0:T(8,128)(2,1)}, u32[]{:S(2)}) copy-start(bf16[512,3840]{1,0:T(8,128)(2,1)} %param.12) | copy-start | bytes 11796484
  76.6 3.0 %copy-start = (bf16[960,3840]{1,0:T(8,128)(2,1)}, bf16[960,3840]{1,0:T(8,128)(2,1)S(1)}, u32[]{:S(2)}) copy-start(bf16[960,3840]{1,0:T(8,128)(2,1)S(1)} %subtract_convert_fusion) | copy-start | bytes 22118404
  85.2 146.0 %reduce-scatter.5.cloned.1.call-start = ((), (), s32[]{:S(2)}) async-start(), calls=%async_computation.2 | async-start | bytes 8110080 | tf_op jit(solution)/shard_map/reduce_scatter | solution.py:84
  130.0 10.4 %collective-permute-start.1 = (f32[4,64,64]{2,1,0:T(8,128)S(1)}, f32[4,64,64]{2,1,0:T(8,128)S(1)}, u32[]{:S(2)}, u32[]{:S(2)}) collective-permute-start(f32[4,64,64]{2,1,0:T(8,128)S(1)} %bitcast.15), channel_id=1, source_target_pairs={{8,0},{16,8},{24,16},{32,24},{40,32},{48,40},{56,48},{64,56},{72,6... | collective-permute-start | bytes 196616 | tf_op jit(solution)/shard_map/ppermute | solution.py:10
Sparse Core Ops, SparseCore 0:
  85.3 42.2 reduce-scatter.6
  132.3 98.8 reduce-scatter.4
where the time goes:
time: 239 us; the launch traced here: 238 us
  waiting for transfers between devices  125 us (52%)
  matrix products  27.9 us (12%)
  blocking collectives  27 us (11%)
  other arithmetic  22 us (9%)
  between operations  14.2 us (6%)
  starting transfers between devices  11.6 us (5%)
  local copies, waits for them, and re-layouts  9.9 us (4%)
    reduce_scatter x1, waiting for transfers between devices, body(): lax.psum_scatter(weight_term, 'dp', scatter_dimension=0, tiled=True)  90.1 us
    unnamed x3, waiting for transfers between devices  32.7 us
    pmax x1, blocking collectives, body(): peak = lax.pmax(jnp.max(logits, axis=1), 'vocab')  16.3 us
    ppermute x2, starting transfers between devices, passed_along(): lax.ppermute(value, axis, [(source, source + steps) for source in range(f...  11.3 us
    psum x1, blocking collectives, body(): total = lax.psum(jnp.sum(expon, axis=1), 'vocab')  10.7 us
    dot_general x1, matrix products, body(): logits = jnp.dot(joint_low, out_weight, preferred_element_type=jnp.float32)  9.64 us
    convert_element_type x1, other arithmetic, body(): grad_low = logit_grad.astype(jnp.bfloat16)  9.6 us
    dot_general x1, matrix products, body(): lax.dot_general(joint_low, grad_low, (((0,), (0,)), ((), ())), preferred_...  9.54 us
  transfers between devices with their start and end apart: 4, of which 3 were waited for; matrix products, arithmetic and copies ran while one was open for 9% of the time, Pallas kernels for 0%

commit v1 on v0

v1 whole, which is shorter than its diff:
```python
import functools

import jax
import jax.numpy as jnp
from jax import lax
from jax.experimental import pallas as pl
from jax.experimental.pallas import tpu as pltpu
from jax.sharding import PartitionSpec as P

MESH = pl.DeviceIdType.MESH
F32 = jnp.float32
BF16 = jnp.bfloat16
KEPT = 5
HALF = 512
WCOLS = 768
LANES = 128


def iota(shape, dim):
    return lax.broadcasted_iota(jnp.int32, shape, dim)


def kernel(
    grid,
    enc_hbm,
    pred_hbm,
    w_hbm,
    futt_hbm,
    pstart_hbm,
    labels_hbm,
    ulen_hbm,
    bocc_hbm,
    locc_hbm,
    fw_hbm,
    gw_ref,
    ge_ref,
    gp_ref,
    enc,
    table,
    w,
    futt,
    pstart,
    labels,
    ulen,
    bocc,
    locc,
    fw,
    aux,
    auxt,
    labrep,
    lrep,
    bl0,
    coef,
    frep,
    picker,
    act32,
    actb,
    actt,
    actp,
    ebuf,
    mx,
    stat,
    ssend,
    srecv,
    scol,
    gbuf,
    hsend,
    hrecv,
    agrad,
    pbuf,
    csend,
    crecv,
    wsum,
    xr1,
    yst,
    yst32,
    yr2,
    yr1,
    xst,
    xst32,
    xr2,
    gpsend,
    gprecv,
    local_sem,
    pred_sem,
    stat_ssem,
    stat_rsem,
    h_ssem,
    h_rsem,
    c_ssem,
    c_rsem,
    p1_ssem,
    p1_rsem,
    p2_ssem,
    p2_rsem,
    gp_sem,
):
    nx, ny, nz = grid
    ndp = nx * ny * 2
    frames = enc.shape[0]
    rows = frames * KEPT
    width, vlocal = w.shape
    own_rows = pred_hbm.shape[0]
    dp = lax.axis_index("dp")
    z = lax.axis_index("vocab")
    cx = dp // (2 * ny)
    cy = lax.rem(dp // 2, ny)
    core = lax.rem(dp, 2)
    wx = nx - 1
    wy = ny - 1

    def zpeer(i):
        return (dp, lax.rem(z + i, nz))

    def xpeer(i):
        return ((lax.rem(cx + i, nx) * ny + cy) * 2 + core, z)

    def ypeer(i):
        return ((cx * ny + lax.rem(cy + i, ny)) * 2 + core, z)

    partner = (dp + 1 - 2 * core, z)
    following = (lax.rem(dp + 1, ndp), z)
    before = (lax.rem(dp + ndp - 1, ndp), z)

    loads = []
    for i, (src, dst) in enumerate(
        (
            (futt_hbm, futt),
            (pstart_hbm, pstart),
            (labels_hbm, labels),
            (ulen_hbm, ulen),
            (bocc_hbm, bocc),
            (locc_hbm, locc),
            (fw_hbm, fw),
            (enc_hbm, enc),
            (pred_hbm, table.at[pl.ds(own_rows, own_rows)]),
            (w_hbm, w),
        )
    ):
        cp = pltpu.make_async_copy(src, dst, local_sem.at[i])
        cp.start()
        loads.append(cp)

    barrier = pltpu.get_barrier_semaphore()
    peers = [zpeer(i) for i in range(1, nz)] + [xpeer(i) for i in range(1, nx)]
    peers += [ypeer(i) for i in range(1, ny)] + [partner, following, before]
    for peer in peers:
        pl.semaphore_signal(barrier, inc=1, device_id=peer, device_id_type=MESH)

    def remote(src, dst, ssem, rsem, peer):
        return pltpu.make_async_remote_copy(
            src_ref=src, dst_ref=dst, send_sem=ssem, recv_sem=rsem, device_id=peer, device_id_type=MESH
        )

    aux[...] = jnp.zeros_like(aux)
    tail = act32.shape[0] - rows
    act32[pl.ds(rows, tail), :] = jnp.zeros((tail, width), F32)
    gbuf[pl.ds(rows, tail), :] = jnp.zeros((tail, vlocal), BF16)
    picker[pl.ds(rows, tail), :] = jnp.zeros((tail, 2 * own_rows), BF16)
    stat[...] = jnp.zeros_like(stat)
    scol[...] = jnp.zeros_like(scol)
    pl.semaphore_wait(barrier, len(peers))
    pred_copy = remote(
        pred_hbm, table.at[pl.ds(0, own_rows)], pred_sem.at[0], pred_sem.at[1], following
    )
    pred_copy.start()

    for cp in loads[:8]:
        cp.wait()
    aux[0:1, 0:frames] = ((futt[...] - (dp - 1) * (own_rows // 64)) * 64 + pstart[...]).astype(F32)
    aux[1:2, 0:frames] = futt[...].astype(F32)
    aux[2:3, 0:frames] = pstart[...].astype(F32)
    aux[8 : 8 + KEPT, 0:frames] = labels[...].astype(F32)
    aux[16 : 16 + KEPT, 0:frames] = fw[...] * bocc[...]
    aux[24 : 24 + KEPT, 0:frames] = fw[...] * locc[...]
    auxt[...] = aux[...].T

    def column(i):
        return auxt[0:frames, i : i + 1]

    utts = ulen.shape[1]
    futt_col = column(1).astype(jnp.int32)
    found = futt_col == iota((frames, utts), 1)
    limit = jnp.sum(jnp.where(found, ulen[...].astype(F32), 0.0), axis=1, keepdims=True)
    start_col = column(2)
    base_col = column(0).astype(jnp.int32)
    lane = iota((frames, LANES), 1)
    first = jnp.logical_and(lane == 0, z == 0)
    table_iota = iota((frames, 2 * own_rows), 1)
    for k in range(KEPT):
        at = pl.ds(k * frames, frames)
        valid = (start_col + float(k) < limit).astype(F32)
        label_coef = column(24 + k) * valid
        blank_coef = column(16 + k)
        labrep[at, :] = jnp.broadcast_to(column(8 + k).astype(jnp.int32) - z * vlocal, (frames, LANES))
        lrep[at, :] = jnp.broadcast_to(label_coef, (frames, LANES))
        bl0[at, :] = jnp.where(first, jnp.broadcast_to(blank_coef, (frames, LANES)), 0.0)
        coef[at, :] = jnp.broadcast_to(blank_coef + label_coef, (frames, LANES))
        picker[at, :] = (base_col + k == table_iota).astype(BF16)

    loads[8].wait()
    pred_copy.wait()
    for k in range(KEPT):
        at = pl.ds(k * frames, frames)
        picked = jnp.dot(picker[at, :], table[...], preferred_element_type=F32)
        act = jnp.tanh(enc[...].astype(F32) + picked)
        act32[at, :] = act
        actb[at, :] = act.astype(BF16)
    share = width // ndp
    for i in range(act32.shape[0] // LANES):
        cols = pl.ds(i * LANES, LANES)
        turned = act32[cols, :].T
        actt[:, cols] = turned
        split = turned.reshape(nx * ny, 2, share, LANES)
        for c in range(2):
            actp[pl.ds(c * (width // 2), width // 2), cols] = (
                split[:, c].reshape(width // 2, LANES).astype(BF16)
            )

    loads[9].wait()

    stat_copies = []
    for h in range(2):
        r0 = h * HALF
        count = min(HALF, rows - r0)
        mx[...] = jnp.full(mx.shape, -jnp.inf, F32)

        def logits_step(c, carry, r0=r0, count=count):
            cols = pl.ds(pl.multiple_of(c * 256, 256), 256)
            block = jnp.dot(actb[pl.ds(r0, count), :], w[:, cols], preferred_element_type=F32)
            ebuf[pl.ds(r0, count), cols] = block
            top = jnp.maximum(block[:, :LANES], block[:, LANES:])
            mx[pl.ds(0, count), :] = jnp.maximum(mx[pl.ds(0, count), :], top)
            return carry

        lax.fori_loop(0, vlocal // 256, logits_step, 0)

        def exp_step(b, carry, r0=r0):
            local = pl.ds(pl.multiple_of(b * 32, 32), 32)
            at = pl.ds(pl.multiple_of(r0 + b * 32, 32), 32)
            peak = jnp.max(mx[local, :], axis=1, keepdims=True)
            wide = jnp.broadcast_to(peak, (32, LANES))
            total = jnp.zeros((32, LANES), F32)
            for t in range(vlocal // LANES):
                cols = pl.ds(t * LANES, LANES)
                e = jnp.exp(ebuf[at, cols] - wide)
                ebuf[at, cols] = e
                total = total + e
            total = jnp.sum(total, axis=1, keepdims=True)
            group = b // 4
            lanes = iota((32, LANES), 1)
            stat[at, :] = jnp.where(lanes == group, peak, jnp.where(lanes == group + 4, total, 0.0))
            return carry

        lax.fori_loop(0, count // 32, exp_step, 0)
        packed = stat[pl.ds(r0, LANES), :]
        for b in range(1, 4):
            packed = packed + stat[pl.ds(r0 + b * LANES, LANES), :]
        ssend[h] = packed.T[0:8, :]
        copies = []
        for i in range(1, nz):
            cp = remote(
                ssend.at[h], srecv.at[h, i - 1], stat_ssem.at[h, i - 1], stat_rsem.at[h, i - 1], zpeer(i)
            )
            cp.start()
            copies.append(cp)
        stat_copies.append(copies)

    h_copies = []
    for h in range(2):
        r0 = h * HALF
        count = min(HALF, rows - r0)
        for cp in stat_copies[h]:
            cp.wait()
        mine = ssend[h]
        peak = mine[0:4]
        for i in range(nz - 1):
            peak = jnp.maximum(peak, srecv[h, i][0:4])
        total = mine[4:8] * jnp.exp(mine[0:4] - peak)
        for i in range(nz - 1):
            got = srecv[h, i]
            total = total + got[4:8] * jnp.exp(got[0:4] - peak)
        scol[0:4, :] = jnp.exp(mine[0:4] - peak) / total
        turned = scol[...].T
        for b in range(4):
            at = pl.ds(r0 + b * LANES, LANES)
            frep[at, :] = jnp.broadcast_to(turned[:, b : b + 1], (LANES, LANES)) * coef[at, :]

        def grad_step(b, carry, r0=r0):
            at = pl.ds(pl.multiple_of(r0 + b * 32, 32), 32)
            scale = frep[at, :]
            label = labrep[at, :]
            lcoef = lrep[at, :]
            lanes = iota((32, LANES), 1)
            for t in range(vlocal // LANES):
                cols = pl.ds(t * LANES, LANES)
                value = ebuf[at, cols] * scale - jnp.where(label - t * LANES == lanes, lcoef, 0.0)
                if t == 0:
                    value = value - bl0[at, :]
                gbuf[at, cols] = value.astype(BF16)
            return carry

        lax.fori_loop(0, count // 32, grad_step, 0)

        def hidden_step(n, carry, r0=r0, h=h):
            at = pl.ds(pl.multiple_of(r0 + n * 256, 256), 256)
            part = lax.dot_general(
                w[...], gbuf[at, :], (((1,), (1,)), ((), ())), preferred_element_type=F32
            )
            hsend[h, :, :, pl.ds(pl.multiple_of(n * 256, 256), 256)] = part.astype(BF16).reshape(
                nz, width // nz, 256
            )
            return carry

        lax.fori_loop(0, HALF // 256, hidden_step, 0)
        copies = []
        for i in sorted(range(1, nz), key=lambda i: -min(i, nz - i)):
            cp = remote(
                hsend.at[h, lax.rem(z + i, nz)],
                hrecv.at[h, i - 1],
                h_ssem.at[h, i - 1],
                h_rsem.at[h, i - 1],
                zpeer(i),
            )
            cp.start()
            copies.append(cp)
        h_copies.append(copies)

    chunks = vlocal // WCOLS
    left = pl.ds(0, WCOLS // 2)
    right = pl.ds(WCOLS // 2, WCOLS // 2)
    half_rows = width // 2
    c_copies, p1_copies, p2_copies = [], [], []
    for step in range(chunks + 3):
        if step < chunks:
            c = step
            slot = c % 2
            pbuf[slot] = jnp.dot(
                actp[...], gbuf[:, pl.ds(c * WCOLS, WCOLS)], preferred_element_type=F32
            )
            theirs = pl.ds(pl.multiple_of((1 - core) * half_rows, half_rows), half_rows)
            csend[c] = pbuf[slot, theirs, :].astype(BF16)
            cp = remote(csend.at[c], crecv.at[c], c_ssem.at[c], c_rsem.at[c], partner)
            cp.start()
            c_copies.append(cp)
        if 1 <= step < chunks + 1:
            c = step - 1
            slot = c % 2
            c_copies[c].wait()
            mine = pl.ds(pl.multiple_of(core * half_rows, half_rows), half_rows)
            both = pbuf[slot, mine, :] + crecv[c].astype(F32)
            wsum[c] = both.astype(BF16).reshape(nx, ny, share, WCOLS)
            copies = []
            for i in range(1, nx):
                cp = remote(
                    wsum.at[c, lax.rem(cx + i, nx), :, :, left],
                    xr1.at[c, i - 1],
                    p1_ssem.at[c, i - 1],
                    p1_rsem.at[c, i - 1],
                    xpeer(i),
                )
                cp.start()
                copies.append(cp)
            for i in range(1, ny):
                cp = remote(
                    wsum.at[c, :, lax.rem(cy + i, ny), :, right],
                    yr1.at[c, i - 1],
                    p1_ssem.at[c, wx + i - 1],
                    p1_rsem.at[c, wx + i - 1],
                    ypeer(i),
                )
                cp.start()
                copies.append(cp)
            p1_copies.append(copies)
        if 2 <= step < chunks + 2:
            c = step - 2
            for cp in p1_copies[c]:
                cp.wait()
            total = wsum[c, cx, :, :, left].astype(F32)
            for i in range(wx):
                total = total + xr1[c, i].astype(F32)
            yst32[c] = total
            yst[c] = total.astype(BF16)
            total = wsum[c, :, cy, :, right].astype(F32)
            for i in range(wy):
                total = total + yr1[c, i].astype(F32)
            xst32[c] = total
            xst[c] = total.astype(BF16)
            copies = []
            for i in range(1, ny):
                cp = remote(
                    yst.at[c, lax.rem(cy + i, ny)],
                    yr2.at[c, i - 1],
                    p2_ssem.at[c, i - 1],
                    p2_rsem.at[c, i - 1],
                    ypeer(i),
                )
                cp.start()
                copies.append(cp)
            for i in range(1, nx):
                cp = remote(
                    xst.at[c, lax.rem(cx + i, nx)],
                    xr2.at[c, i - 1],
                    p2_ssem.at[c, wy + i - 1],
                    p2_rsem.at[c, wy + i - 1],
                    xpeer(i),
                )
                cp.start()
                copies.append(cp)
            p2_copies.append(copies)
        if step >= 3:
            c = step - 3
            for cp in p2_copies[c]:
                cp.wait()
            total = yst32[c, cy]
            for i in range(wy):
                total = total + yr2[c, i].astype(F32)
            gw_ref[:, pl.ds(c * WCOLS, WCOLS // 2)] = total
            total = xst32[c, cx]
            for i in range(wx):
                total = total + xr2[c, i].astype(F32)
            gw_ref[:, pl.ds(c * WCOLS + WCOLS // 2, WCOLS // 2)] = total

    slice_rows = width // nz
    act_at = pl.ds(pl.multiple_of(z * slice_rows, slice_rows), slice_rows)
    for h in range(2):
        cols = pl.ds(h * HALF, HALF)
        for cp in h_copies[h]:
            cp.wait()
        total = hsend[h, z].astype(F32)
        for i in range(nz - 1):
            total = total + hrecv[h, i].astype(F32)
        act = actt[act_at, cols]
        agrad[:, cols] = total * (1.0 - act * act)
    grads = agrad[...]
    summed = grads[:, 0:frames]
    for k in range(1, KEPT):
        summed = summed + grads[:, k * frames : (k + 1) * frames]
    ge_ref[...] = summed
    high = grads.astype(BF16)
    low = (grads - high.astype(F32)).astype(BF16)
    slots = jnp.dot(high, picker[...], preferred_element_type=F32) + jnp.dot(
        low, picker[...], preferred_element_type=F32
    )
    gpsend[...] = slots[:, 0:own_rows]
    gp_copy = remote(gpsend, gprecv, gp_sem.at[0], gp_sem.at[1], before)
    gp_copy.start()
    gp_copy.wait()
    gp_ref[...] = (slots[:, own_rows:] + gprecv[...]).T


def body(grid, enc, pred, w, futt, pstart, labels, ulen, bocc, locc, fw):
    nx, ny, nz = grid
    frames, width = enc.shape
    vlocal = w.shape[1]
    slots, depth, _ = pred.shape
    own_rows = slots * depth
    rows_pad = 2 * HALF
    share = width // (nx * ny * 2)
    utts = ulen.shape[0]
    chunks = vlocal // WCOLS
    hw = WCOLS // 2
    vm = pltpu.VMEM
    dma = pltpu.SemaphoreType.DMA
    i32 = jnp.int32
    scratch = [
        vm((frames, width), BF16),
        vm((2 * own_rows, width), BF16),
        vm((width, vlocal), BF16),
        vm((1, frames), i32),
        vm((1, frames), i32),
        vm((KEPT, frames), i32),
        vm((1, utts), i32),
        vm((KEPT, frames), F32),
        vm((KEPT, frames), F32),
        vm((1, frames), F32),
        vm((LANES, 2 * LANES), F32),
        vm((2 * LANES, LANES), F32),
        vm((rows_pad, LANES), i32),
        vm((rows_pad, LANES), F32),
        vm((rows_pad, LANES), F32),
        vm((rows_pad, LANES), F32),
        vm((rows_pad, LANES), F32),
        vm((rows_pad, 2 * own_rows), BF16),
        vm((rows_pad, width), F32),
        vm((rows_pad, width), BF16),
        vm((width, rows_pad), F32),
        vm((width, rows_pad), BF16),
        vm((frames * KEPT, vlocal), F32),
        vm((HALF, LANES), F32),
        vm((rows_pad, LANES), F32),
        vm((2, 8, LANES), F32),
        vm((2, nz - 1, 8, LANES), F32),
        vm((LANES, LANES), F32),
        vm((rows_pad, vlocal), BF16),
        vm((2, nz, width // nz, HALF), BF16),
        vm((2, nz - 1, width // nz, HALF), BF16),
        vm((width // nz, rows_pad), F32),
        vm((2, width, WCOLS), F32),
        vm((chunks, width // 2, WCOLS), BF16),
        vm((chunks, width // 2, WCOLS), BF16),
        vm((chunks, nx, ny, share, WCOLS), BF16),
        vm((chunks, nx - 1, ny, share, hw), BF16),
        vm((chunks, ny, share, hw), BF16),
        vm((chunks, ny, share, hw), F32),
        vm((chunks, ny - 1, share, hw), BF16),
        vm((chunks, ny - 1, nx, share, hw), BF16),
        vm((chunks, nx, share, hw), BF16),
        vm((chunks, nx, share, hw), F32),
        vm((chunks, nx - 1, share, hw), BF16),
        vm((width // nz, own_rows), F32),
        vm((width // nz, own_rows), F32),
        dma((10,)),
        dma((2,)),
        dma((2, nz - 1)),
        dma((2, nz - 1)),
        dma((2, nz - 1)),
        dma((2, nz - 1)),
        dma((chunks,)),
        dma((chunks,)),
        dma((chunks, nx + ny - 2)),
        dma((chunks, nx + ny - 2)),
        dma((chunks, nx + ny - 2)),
        dma((chunks, nx + ny - 2)),
        dma((2,)),
    ]
    gw, ge, gp = pl.pallas_call(
        functools.partial(kernel, grid),
        out_shape=(
            jax.ShapeDtypeStruct((share, vlocal), F32),
            jax.ShapeDtypeStruct((width // nz, frames), F32),
            jax.ShapeDtypeStruct((own_rows, width // nz), F32),
        ),
        in_specs=[pl.BlockSpec(memory_space=pl.ANY)] * 10,
        out_specs=[pl.BlockSpec(memory_space=pltpu.VMEM)] * 3,
        scratch_shapes=scratch,
        compiler_params=pltpu.CompilerParams(
            collective_id=0, has_side_effects=True, vmem_limit_bytes=60 * 2**20
        ),
    )(
        enc,
        pred.reshape(own_rows, width),
        w,
        futt.reshape(1, frames),
        pstart.reshape(1, frames),
        labels.T,
        ulen.reshape(1, utts),
        bocc.T,
        locc.T,
        fw.reshape(1, frames),
    )
    return gw, ge.T, gp.reshape(slots, depth, width // nz)


def solution(mesh, sizes=(4, 4)):
    grid = (sizes[0], sizes[1], mesh.shape["vocab"])
    in_specs = (
        P("dp", None),
        P("dp", None, None),
        P(None, "vocab"),
        P("dp"),
        P("dp"),
        P("dp", None),
        P(),
        P("dp", None),
        P("dp", None),
        P("dp"),
    )
    out_specs = (P("dp", "vocab"), P("dp", "vocab"), P("dp", None, "vocab"))
    return jax.shard_map(
        functools.partial(body, grid), mesh=mesh, in_specs=in_specs, out_specs=out_specs, check_vma=False
    )
```

time: 239 us -> 79.1 us (0.33)
  waiting for transfers between devices: 125 us -> 0 us
  Pallas kernels: 0 us -> 73.6 us
  matrix products: 27.9 us -> 0 us
  blocking collectives: 27 us -> 0 us
  other arithmetic: 22 us -> 0 us
  between operations: 14.2 us -> 0.64 us
  starting transfers between devices: 11.6 us -> 0 us
  local copies, waits for them, and re-layouts: 9.9 us -> 4.69 us
    reduce_scatter x1 -> x0, waiting for transfers between devices: 90.1 us -> none  [body(): lax.psum_scatter(weight_term, 'dp', scatter_dimension=0, tiled=True)]
    pallas_call x0 -> x1, Pallas kernels: none -> 73.6 us  [body(): pl.pallas_call(functools.partial(kernel, grid), out_shape=(jax.ShapeDtype...]
    unnamed x3 -> x0, waiting for transfers between devices: 32.7 us -> none
    dot_general x4 -> x0, matrix products: 22.3 us -> none  [the longest x1 9.64 us: body(): logits = jnp.dot(joint_low, out_weight, preferred_element_type=jnp.float32)]
    pmax x1 -> x0, blocking collectives: 16.3 us -> none  [body(): peak = lax.pmax(jnp.max(logits, axis=1), 'vocab')]
    ppermute x2 -> x0, starting transfers between devices: 11.3 us -> none  [passed_along(): lax.ppermute(value, axis, [(source, source + steps) for source in range(f...]
    psum x1 -> x0, blocking collectives: 10.7 us -> none  [body(): total = lax.psum(jnp.sum(expon, axis=1), 'vocab')]
    convert_element_type x2 -> x0, other arithmetic: 9.61 us -> none  [the longest x1 9.6 us: body(): grad_low = logit_grad.astype(jnp.bfloat16)]
  transfers between devices with their start and end apart: 4 -> 0, of which waited for: 3 -> 0; matrix products, arithmetic and copies ran while one was open for 9% -> 0% of each run, Pallas kernels for 0% -> 0%
where the time goes in v1:
time: 79.1 us; the launch traced here: 78.9 us
  Pallas kernels  73.6 us (93%)
  local copies, waits for them, and re-layouts  4.69 us (6%)
    pallas_call x1, Pallas kernels, body(): pl.pallas_call(functools.partial(kernel, grid), out_shape=(jax.ShapeDtype...  73.6 us
    unnamed x3, local copies, waits for them, and re-layouts  4.69 us

profile of v1, /device:TPU:1, one launch (start us, length us, event | category | flops | bytes accessed | tf_op | source)
XLA Modules:
  0.0 78.9 jit_solution(17516969004304912854)
XLA Ops:
  0.6 73.6 %shard_map.121 = (f32[16,3840]{1,0:T(8,128)}, f32[64,192]{1,0:T(8,128)}, f32[256,64]{1,0:T(8,128)}) custom-call(bf16[192,512]{1,0:T(8,128)(2,1)} %enc_hbm.1, bf16[256,512]{1,0:T(8,128)(2,1)} %bitcast.10, bf16[512,3840]{1,0:T(8,128)(2,1)} %w_hbm.1, s32[1,192]{1,0:T(1,128)} %bitcast.16, s32[1,192]{1,0:T(1,128)} %bitcast.17, s32[5,192]{1,0:T(8,128)} %bitcast.13, ...), custom_call_target="tpu_custom_call" | custom-call | tf_op jit(solution)/shard_map/pallas_call | solution.py:527
  74.2 1.7 %copy.16 = f32[16,3840]{1,0:T(8,128)} copy(f32[16,3840]{1,0:T(8,128)} %get-tuple-element.12) | data formatting | bytes 491520
  75.9 1.5 %copy.17 = f32[192,64]{0,1:T(8,128)} copy(f32[192,64]{0,1:T(8,128)} %bitcast.12) | data formatting | bytes 98304
  77.4 1.6 %copy.18 = f32[4,64,64]{2,1,0:T(8,128)} copy(f32[4,64,64]{2,1,0:T(8,128)} %bitcast.11) | data formatting | bytes 131072

commit v2 on v1

--- a/solution.py
+++ b/solution.py
@@ -13,6 +13,8 @@
 KEPT = 5
 HALF = 512
 WCOLS = 768
+LCOLS = 1280
+EROWS = 64
 LANES = 128
 
 
@@ -59,6 +61,7 @@
     actp,
     ebuf,
     mx,
+    sums,
     stat,
     ssend,
     srecv,
@@ -226,33 +229,39 @@
         mx[...] = jnp.full(mx.shape, -jnp.inf, F32)
 
         def logits_step(c, carry, r0=r0, count=count):
-            cols = pl.ds(pl.multiple_of(c * 256, 256), 256)
+            cols = pl.ds(pl.multiple_of(c * LCOLS, LCOLS), LCOLS)
             block = jnp.dot(actb[pl.ds(r0, count), :], w[:, cols], preferred_element_type=F32)
             ebuf[pl.ds(r0, count), cols] = block
-            top = jnp.maximum(block[:, :LANES], block[:, LANES:])
-            mx[pl.ds(0, count), :] = jnp.maximum(mx[pl.ds(0, count), :], top)
+            top = mx[pl.ds(0, count), :]
+            for t in range(LCOLS // LANES):
+                top = jnp.maximum(top, block[:, t * LANES : (t + 1) * LANES])
+            mx[pl.ds(0, count), :] = top
             return carry
 
-        lax.fori_loop(0, vlocal // 256, logits_step, 0)
+        lax.fori_loop(0, vlocal // LCOLS, logits_step, 0)
+        peaks = jnp.max(mx[pl.ds(0, count), :], axis=1, keepdims=True)
+        mx[pl.ds(0, count), :] = jnp.broadcast_to(peaks, (count, LANES))
 
         def exp_step(b, carry, r0=r0):
-            local = pl.ds(pl.multiple_of(b * 32, 32), 32)
-            at = pl.ds(pl.multiple_of(r0 + b * 32, 32), 32)
-            peak = jnp.max(mx[local, :], axis=1, keepdims=True)
-            wide = jnp.broadcast_to(peak, (32, LANES))
-            total = jnp.zeros((32, LANES), F32)
+            local = pl.ds(pl.multiple_of(b * EROWS, EROWS), EROWS)
+            at = pl.ds(pl.multiple_of(r0 + b * EROWS, EROWS), EROWS)
+            wide = mx[local, :]
+            total = jnp.zeros((EROWS, LANES), F32)
             for t in range(vlocal // LANES):
                 cols = pl.ds(t * LANES, LANES)
                 e = jnp.exp(ebuf[at, cols] - wide)
                 ebuf[at, cols] = e
                 total = total + e
-            total = jnp.sum(total, axis=1, keepdims=True)
-            group = b // 4
-            lanes = iota((32, LANES), 1)
-            stat[at, :] = jnp.where(lanes == group, peak, jnp.where(lanes == group + 4, total, 0.0))
+            sums[local, :] = total
             return carry
 
-        lax.fori_loop(0, count // 32, exp_step, 0)
+        lax.fori_loop(0, count // EROWS, exp_step, 0)
+        totals = jnp.sum(sums[pl.ds(0, count), :], axis=1, keepdims=True)
+        group = iota((count, LANES), 0) // LANES
+        lanes = iota((count, LANES), 1)
+        stat[pl.ds(r0, count), :] = jnp.where(
+            lanes == group, mx[pl.ds(0, count), :], jnp.where(lanes == group + 4, totals, 0.0)
+        )
         packed = stat[pl.ds(r0, LANES), :]
         for b in range(1, 4):
             packed = packed + stat[pl.ds(r0 + b * LANES, LANES), :]
@@ -302,17 +311,10 @@
 
         lax.fori_loop(0, count // 32, grad_step, 0)
 
-        def hidden_step(n, carry, r0=r0, h=h):
-            at = pl.ds(pl.multiple_of(r0 + n * 256, 256), 256)
-            part = lax.dot_general(
-                w[...], gbuf[at, :], (((1,), (1,)), ((), ())), preferred_element_type=F32
-            )
-            hsend[h, :, :, pl.ds(pl.multiple_of(n * 256, 256), 256)] = part.astype(BF16).reshape(
-                nz, width // nz, 256
-            )
-            return carry
-
-        lax.fori_loop(0, HALF // 256, hidden_step, 0)
+        part = lax.dot_general(
+            w[...], gbuf[pl.ds(r0, HALF), :], (((1,), (1,)), ((), ())), preferred_element_type=F32
+        )
+        hsend[h] = part.astype(BF16).reshape(nz, width // nz, HALF)
         copies = []
         for i in sorted(range(1, nz), key=lambda i: -min(i, nz - i)):
             cp = remote(
@@ -372,6 +374,31 @@
                 cp.start()
                 copies.append(cp)
             p1_copies.append(copies)
+        if step == chunks:
+            slice_rows = width // nz
+            act_at = pl.ds(pl.multiple_of(z * slice_rows, slice_rows), slice_rows)
+            for h in range(2):
+                cols = pl.ds(h * HALF, HALF)
+                for cp in h_copies[h]:
+                    cp.wait()
+                total = hsend[h, z].astype(F32)
+                for i in range(nz - 1):
+                    total = total + hrecv[h, i].astype(F32)
+                act = actt[act_at, cols]
+                agrad[:, cols] = total * (1.0 - act * act)
+            grads = agrad[...]
+            summed = grads[:, 0:frames]
+            for k in range(1, KEPT):
+                summed = summed + grads[:, k * frames : (k + 1) * frames]
+            ge_ref[...] = summed
+            high = grads.astype(BF16)
+            low = (grads - high.astype(F32)).astype(BF16)
+            slots = jnp.dot(high, picker[...], preferred_element_type=F32) + jnp.dot(
+                low, picker[...], preferred_element_type=F32
+            )
+            gpsend[...] = slots[:, 0:own_rows]
+            gp_copy = remote(gpsend, gprecv, gp_sem.at[0], gp_sem.at[1], before)
+            gp_copy.start()
         if 2 <= step < chunks + 2:
             c = step - 2
             for cp in p1_copies[c]:
@@ -421,32 +448,17 @@
                 total = total + xr2[c, i].astype(F32)
             gw_ref[:, pl.ds(c * WCOLS + WCOLS // 2, WCOLS // 2)] = total
 
-    slice_rows = width // nz
-    act_at = pl.ds(pl.multiple_of(z * slice_rows, slice_rows), slice_rows)
-    for h in range(2):
-        cols = pl.ds(h * HALF, HALF)
-        for cp in h_copies[h]:
-            cp.wait()
-        total = hsend[h, z].astype(F32)
-        for i in range(nz - 1):
-            total = total + hrecv[h, i].astype(F32)
-        act = actt[act_at, cols]
-        agrad[:, cols] = total * (1.0 - act * act)
-    grads = agrad[...]
-    summed = grads[:, 0:frames]
-    for k in range(1, KEPT):
-        summed = summed + grads[:, k * frames : (k + 1) * frames]
-    ge_ref[...] = summed
-    high = grads.astype(BF16)
-    low = (grads - high.astype(F32)).astype(BF16)
-    slots = jnp.dot(high, picker[...], preferred_element_type=F32) + jnp.dot(
-        low, picker[...], preferred_element_type=F32
-    )
-    gpsend[...] = slots[:, 0:own_rows]
-    gp_copy = remote(gpsend, gprecv, gp_sem.at[0], gp_sem.at[1], before)
-    gp_copy.start()
     gp_copy.wait()
     gp_ref[...] = (slots[:, own_rows:] + gprecv[...]).T
+
+
+def handover(*refs):
+    sems = refs[6]
+    copies = [pltpu.make_async_copy(refs[i], refs[3 + i], sems.at[i]) for i in range(3)]
+    for cp in copies:
+        cp.start()
+    for cp in copies:
+        cp.wait()
 
 
 def body(grid, enc, pred, w, futt, pstart, labels, ulen, bocc, locc, fw):
@@ -488,6 +500,7 @@
         vm((width, rows_pad), BF16),
         vm((frames * KEPT, vlocal), F32),
         vm((HALF, LANES), F32),
+        vm((HALF, LANES), F32),
         vm((rows_pad, LANES), F32),
         vm((2, 8, LANES), F32),
         vm((2, nz - 1, 8, LANES), F32),
@@ -524,7 +537,7 @@
         dma((chunks, nx + ny - 2)),
         dma((2,)),
     ]
-    gw, ge, gp = pl.pallas_call(
+    results = pl.pallas_call(
         functools.partial(kernel, grid),
         out_shape=(
             jax.ShapeDtypeStruct((share, vlocal), F32),
@@ -549,6 +562,13 @@
         locc.T,
         fw.reshape(1, frames),
     )
+    gw, ge, gp = pl.pallas_call(
+        handover,
+        out_shape=tuple(jax.ShapeDtypeStruct(r.shape, r.dtype) for r in results),
+        in_specs=[pl.BlockSpec(memory_space=pltpu.VMEM)] * 3,
+        out_specs=[pl.BlockSpec(memory_space=pl.ANY)] * 3,
+        scratch_shapes=[dma((3,))],
+    )(*results)
     return gw, ge.T, gp.reshape(slots, depth, width // nz)
 
 

time: 79.1 us -> 63.8 us (0.81)
  Pallas kernels: 73.6 us -> 62.9 us
  local copies, waits for them, and re-layouts: 4.69 us -> 0 us
    pallas_call x1, Pallas kernels: 73.6 us -> 61.1 us  [body(): pl.pallas_call(functools.partial(kernel, grid), out_shape=(jax.ShapeDtype...]
    unnamed x3 -> x0, local copies, waits for them, and re-layouts: 4.69 us -> none
    pallas_call x0 -> x1, Pallas kernels: none -> 1.84 us  [body(): pl.pallas_call(handover, out_shape=tuple((jax.ShapeDtypeStruct(r.shape, r...]
where the time goes in v2:
time: 63.8 us; the launch traced here: 63.7 us
  Pallas kernels  62.9 us (99%)
  between operations  0.8 us (1%)
    pallas_call x1, Pallas kernels, body(): pl.pallas_call(functools.partial(kernel, grid), out_shape=(jax.ShapeDtype...  61.1 us
    pallas_call x1, Pallas kernels, body(): pl.pallas_call(handover, out_shape=tuple((jax.ShapeDtypeStruct(r.shape, r...  1.84 us

profile of v2, /device:TPU:1, one launch (start us, length us, event | category | flops | bytes accessed | tf_op | source)
XLA Modules:
  0.0 63.7 jit_solution(7374040930287699254)
XLA Ops:
  0.6 61.1 %shard_map.121 = (f32[16,3840]{1,0:T(8,128)}, f32[64,192]{1,0:T(8,128)}, f32[256,64]{1,0:T(8,128)}) custom-call(bf16[192,512]{1,0:T(8,128)(2,1)} %enc_hbm.1, bf16[256,512]{1,0:T(8,128)(2,1)} %bitcast.10, bf16[512,3840]{1,0:T(8,128)(2,1)} %w_hbm.1, s32[1,192]{1,0:T(1,128)} %bitcast.14, s32[1,192]{1,0:T(1,128)} %bitcast.15, s32[5,192]{1,0:T(8,128)} %bitcast.11, ...), custom_call_target="tpu_custom_call" | custom-call | tf_op jit(solution)/shard_map/pallas_call | solution.py:540
  61.7 1.8 %shard_map.122 = (f32[16,3840]{1,0:T(8,128)}, f32[64,192]{1,0:T(8,128)}, f32[256,64]{1,0:T(8,128)}) custom-call(f32[16,3840]{1,0:T(8,128)} %get-tuple-element.9.refs_0_, f32[64,192]{1,0:T(8,128)} %get-tuple-element.10.refs_1_, f32[256,64]{1,0:T(8,128)} %get-tuple-element.11.refs_2_), custom_call_target="tpu_custom_call" | custom-call | tf_op jit(solution)/shard_map/pallas_call | solution.py:565

commit v3 on v2

--- a/solution.py
+++ b/solution.py
@@ -68,7 +68,11 @@
     scol,
     gbuf,
     hsend,
-    hrecv,
+    far,
+    half_far,
+    near,
+    relayed,
+    rsend,
     agrad,
     pbuf,
     csend,
@@ -275,8 +279,9 @@
             copies.append(cp)
         stat_copies.append(copies)
 
-    h_copies = []
-    for h in range(2):
+    slice_rows = width // nz
+
+    def grad_half(h):
         r0 = h * HALF
         count = min(HALF, rows - r0)
         for cp in stat_copies[h]:
@@ -295,7 +300,7 @@
             at = pl.ds(r0 + b * LANES, LANES)
             frep[at, :] = jnp.broadcast_to(turned[:, b : b + 1], (LANES, LANES)) * coef[at, :]
 
-        def grad_step(b, carry, r0=r0):
+        def grad_step(b, carry):
             at = pl.ds(pl.multiple_of(r0 + b * 32, 32), 32)
             scale = frep[at, :]
             label = labrep[at, :]
@@ -311,143 +316,194 @@
 
         lax.fori_loop(0, count // 32, grad_step, 0)
 
+    h_copies = {}
+    relay_copies = {}
+
+    def hidden_half(h):
+        r0 = h * HALF
         part = lax.dot_general(
             w[...], gbuf[pl.ds(r0, HALF), :], (((1,), (1,)), ((), ())), preferred_element_type=F32
         )
-        hsend[h] = part.astype(BF16).reshape(nz, width // nz, HALF)
+        hsend[h] = part.astype(BF16).reshape(nz, slice_rows, HALF)
         copies = []
-        for i in sorted(range(1, nz), key=lambda i: -min(i, nz - i)):
+        quarter = HALF // 2
+        plan = [
+            (hsend.at[h, lax.rem(z + 4, nz), :, pl.ds(0, quarter)], half_far.at[h, 0], 2),
+            (hsend.at[h, lax.rem(z + 4, nz), :, pl.ds(quarter, quarter)], half_far.at[h, 1], nz - 2),
+            (hsend.at[h, lax.rem(z + 3, nz)], far.at[h, 0], 1),
+            (hsend.at[h, lax.rem(z + nz - 3, nz)], far.at[h, 1], nz - 1),
+            (hsend.at[h, lax.rem(z + 1, nz)], near.at[h, 0], 1),
+            (hsend.at[h, lax.rem(z + nz - 1, nz)], near.at[h, 1], nz - 1),
+        ]
+        for n, (src, dst, shift) in enumerate(plan):
+            cp = remote(src, dst, h_ssem.at[h, n], h_rsem.at[h, n], zpeer(shift))
+            cp.start()
+            copies.append(cp)
+        h_copies[h] = copies
+
+    def relay_half(h):
+        copies = []
+        quarter = HALF // 2
+        for side, shift in ((0, 2), (1, nz - 2)):
+            h_copies[h][side].wait()
+            h_copies[h][2 + side].wait()
+            own = lax.rem(z + shift, nz)
+            for part in range(2):
+                cols = pl.ds(part * quarter, quarter)
+                total = hsend[h, own, :, cols].astype(F32) + far[h, side, :, cols].astype(F32)
+                if part == side:
+                    total = total + half_far[h, side].astype(F32)
+                rsend[h, side, :, cols] = total.astype(BF16)
             cp = remote(
-                hsend.at[h, lax.rem(z + i, nz)],
-                hrecv.at[h, i - 1],
-                h_ssem.at[h, i - 1],
-                h_rsem.at[h, i - 1],
-                zpeer(i),
+                rsend.at[h, side],
+                relayed.at[h, side],
+                h_ssem.at[h, 6 + side],
+                h_rsem.at[h, 6 + side],
+                zpeer(shift),
             )
             cp.start()
             copies.append(cp)
-        h_copies.append(copies)
+        relay_copies[h] = copies
+
+    def hidden_finish():
+        act_at = pl.ds(pl.multiple_of(z * slice_rows, slice_rows), slice_rows)
+        for h in range(2):
+            cols = pl.ds(h * HALF, HALF)
+            for cp in h_copies[h][4:] + relay_copies[h]:
+                cp.wait()
+            total = hsend[h, z].astype(F32)
+            for i in range(2):
+                total = total + near[h, i].astype(F32) + relayed[h, i].astype(F32)
+            act = actt[act_at, cols]
+            agrad[:, cols] = total * (1.0 - act * act)
+        grads = agrad[...]
+        summed = grads[:, 0:frames]
+        for k in range(1, KEPT):
+            summed = summed + grads[:, k * frames : (k + 1) * frames]
+        ge_ref[...] = summed
+        high = grads.astype(BF16)
+        low = (grads - high.astype(F32)).astype(BF16)
+        slots = jnp.dot(high, picker[...], preferred_element_type=F32) + jnp.dot(
+            low, picker[...], preferred_element_type=F32
+        )
+        gpsend[...] = slots[:, 0:own_rows]
+        gp_copy = remote(gpsend, gprecv, gp_sem.at[0], gp_sem.at[1], before)
+        gp_copy.start()
+        return slots, gp_copy
 
     chunks = vlocal // WCOLS
     left = pl.ds(0, WCOLS // 2)
     right = pl.ds(WCOLS // 2, WCOLS // 2)
     half_rows = width // 2
-    c_copies, p1_copies, p2_copies = [], [], []
-    for step in range(chunks + 3):
-        if step < chunks:
-            c = step
-            slot = c % 2
-            pbuf[slot] = jnp.dot(
-                actp[...], gbuf[:, pl.ds(c * WCOLS, WCOLS)], preferred_element_type=F32
+    c_copies, p1_copies, p2_copies = {}, {}, {}
+
+    def weight_chunk(c):
+        slot = c % 3
+        pbuf[slot] = jnp.dot(
+            actp[...], gbuf[:, pl.ds(c * WCOLS, WCOLS)], preferred_element_type=F32
+        )
+        theirs = pl.ds(pl.multiple_of((1 - core) * half_rows, half_rows), half_rows)
+        csend[c] = pbuf[slot, theirs, :].astype(BF16)
+        cp = remote(csend.at[c], crecv.at[c], c_ssem.at[c], c_rsem.at[c], partner)
+        cp.start()
+        c_copies[c] = cp
+
+    def weight_first(c):
+        c_copies[c].wait()
+        mine = pl.ds(pl.multiple_of(core * half_rows, half_rows), half_rows)
+        both = pbuf[c % 3, mine, :] + crecv[c].astype(F32)
+        wsum[c] = both.astype(BF16).reshape(nx, ny, share, WCOLS)
+        copies = []
+        for i in sorted(range(1, nx), key=lambda i: -min(i, nx - i)):
+            cp = remote(
+                wsum.at[c, lax.rem(cx + i, nx), :, :, left],
+                xr1.at[c, i - 1],
+                p1_ssem.at[c, i - 1],
+                p1_rsem.at[c, i - 1],
+                xpeer(i),
             )
-            theirs = pl.ds(pl.multiple_of((1 - core) * half_rows, half_rows), half_rows)
-            csend[c] = pbuf[slot, theirs, :].astype(BF16)
-            cp = remote(csend.at[c], crecv.at[c], c_ssem.at[c], c_rsem.at[c], partner)
             cp.start()
-            c_copies.append(cp)
-        if 1 <= step < chunks + 1:
-            c = step - 1
-            slot = c % 2
-            c_copies[c].wait()
-            mine = pl.ds(pl.multiple_of(core * half_rows, half_rows), half_rows)
-            both = pbuf[slot, mine, :] + crecv[c].astype(F32)
-            wsum[c] = both.astype(BF16).reshape(nx, ny, share, WCOLS)
-            copies = []
-            for i in range(1, nx):
-                cp = remote(
-                    wsum.at[c, lax.rem(cx + i, nx), :, :, left],
-                    xr1.at[c, i - 1],
-                    p1_ssem.at[c, i - 1],
-                    p1_rsem.at[c, i - 1],
-                    xpeer(i),
-                )
-                cp.start()
-                copies.append(cp)
-            for i in range(1, ny):
-                cp = remote(
-                    wsum.at[c, :, lax.rem(cy + i, ny), :, right],
-                    yr1.at[c, i - 1],
-                    p1_ssem.at[c, wx + i - 1],
-                    p1_rsem.at[c, wx + i - 1],
-                    ypeer(i),
-                )
-                cp.start()
-                copies.append(cp)
-            p1_copies.append(copies)
-        if step == chunks:
-            slice_rows = width // nz
-            act_at = pl.ds(pl.multiple_of(z * slice_rows, slice_rows), slice_rows)
-            for h in range(2):
-                cols = pl.ds(h * HALF, HALF)
-                for cp in h_copies[h]:
-                    cp.wait()
-                total = hsend[h, z].astype(F32)
-                for i in range(nz - 1):
-                    total = total + hrecv[h, i].astype(F32)
-                act = actt[act_at, cols]
-                agrad[:, cols] = total * (1.0 - act * act)
-            grads = agrad[...]
-            summed = grads[:, 0:frames]
-            for k in range(1, KEPT):
-                summed = summed + grads[:, k * frames : (k + 1) * frames]
-            ge_ref[...] = summed
-            high = grads.astype(BF16)
-            low = (grads - high.astype(F32)).astype(BF16)
-            slots = jnp.dot(high, picker[...], preferred_element_type=F32) + jnp.dot(
-                low, picker[...], preferred_element_type=F32
+            copies.append(cp)
+        for i in sorted(range(1, ny), key=lambda i: -min(i, ny - i)):
+            cp = remote(
+                wsum.at[c, :, lax.rem(cy + i, ny), :, right],
+                yr1.at[c, i - 1],
+                p1_ssem.at[c, wx + i - 1],
+                p1_rsem.at[c, wx + i - 1],
+                ypeer(i),
             )
-            gpsend[...] = slots[:, 0:own_rows]
-            gp_copy = remote(gpsend, gprecv, gp_sem.at[0], gp_sem.at[1], before)
-            gp_copy.start()
-        if 2 <= step < chunks + 2:
-            c = step - 2
-            for cp in p1_copies[c]:
-                cp.wait()
-            total = wsum[c, cx, :, :, left].astype(F32)
-            for i in range(wx):
-                total = total + xr1[c, i].astype(F32)
-            yst32[c] = total
-            yst[c] = total.astype(BF16)
-            total = wsum[c, :, cy, :, right].astype(F32)
-            for i in range(wy):
-                total = total + yr1[c, i].astype(F32)
-            xst32[c] = total
-            xst[c] = total.astype(BF16)
-            copies = []
-            for i in range(1, ny):
-                cp = remote(
-                    yst.at[c, lax.rem(cy + i, ny)],
-                    yr2.at[c, i - 1],
-                    p2_ssem.at[c, i - 1],
-                    p2_rsem.at[c, i - 1],
-                    ypeer(i),
-                )
-                cp.start()
-                copies.append(cp)
-            for i in range(1, nx):
-                cp = remote(
-                    xst.at[c, lax.rem(cx + i, nx)],
-                    xr2.at[c, i - 1],
-                    p2_ssem.at[c, wy + i - 1],
-                    p2_rsem.at[c, wy + i - 1],
-                    xpeer(i),
-                )
-                cp.start()
-                copies.append(cp)
-            p2_copies.append(copies)
-        if step >= 3:
-            c = step - 3
-            for cp in p2_copies[c]:
-                cp.wait()
-            total = yst32[c, cy]
-            for i in range(wy):
-                total = total + yr2[c, i].astype(F32)
-            gw_ref[:, pl.ds(c * WCOLS, WCOLS // 2)] = total
-            total = xst32[c, cx]
-            for i in range(wx):
-                total = total + xr2[c, i].astype(F32)
-            gw_ref[:, pl.ds(c * WCOLS + WCOLS // 2, WCOLS // 2)] = total
-
+            cp.start()
+            copies.append(cp)
+        p1_copies[c] = copies
+
+    def weight_second(c):
+        for cp in p1_copies[c]:
+            cp.wait()
+        total = wsum[c, cx, :, :, left].astype(F32)
+        for i in range(wx):
+            total = total + xr1[c, i].astype(F32)
+        yst32[c] = total
+        yst[c] = total.astype(BF16)
+        total = wsum[c, :, cy, :, right].astype(F32)
+        for i in range(wy):
+            total = total + yr1[c, i].astype(F32)
+        xst32[c] = total
+        xst[c] = total.astype(BF16)
+        copies = []
+        for i in range(1, ny):
+            cp = remote(
+                yst.at[c, lax.rem(cy + i, ny)],
+                yr2.at[c, i - 1],
+                p2_ssem.at[c, i - 1],
+                p2_rsem.at[c, i - 1],
+                ypeer(i),
+            )
+            cp.start()
+            copies.append(cp)
+        for i in range(1, nx):
+            cp = remote(
+                xst.at[c, lax.rem(cx + i, nx)],
+                xr2.at[c, i - 1],
+                p2_ssem.at[c, wy + i - 1],
+                p2_rsem.at[c, wy + i - 1],
+                xpeer(i),
+            )
+            cp.start()
+            copies.append(cp)
+        p2_copies[c] = copies
+
+    def weight_last(c):
+        for cp in p2_copies[c]:
+            cp.wait()
+        total = yst32[c, cy]
+        for i in range(wy):
+            total = total + yr2[c, i].astype(F32)
+        gw_ref[:, pl.ds(c * WCOLS, WCOLS // 2)] = total
+        total = xst32[c, cx]
+        for i in range(wx):
+            total = total + xr2[c, i].astype(F32)
+        gw_ref[:, pl.ds(c * WCOLS + WCOLS // 2, WCOLS // 2)] = total
+
+    grad_half(0)
+    hidden_half(0)
+    grad_half(1)
+    weight_chunk(0)
+    weight_chunk(1)
+    weight_first(0)
+    hidden_half(1)
+    relay_half(0)
+    for c in range(2, chunks):
+        weight_chunk(c)
+        weight_first(c - 1)
+    weight_second(0)
+    weight_first(chunks - 1)
+    relay_half(1)
+    for c in range(1, chunks - 1):
+        weight_second(c)
+    slots, gp_copy = hidden_finish()
+    weight_second(chunks - 1)
+    for c in range(chunks):
+        weight_last(c)
     gp_copy.wait()
     gp_ref[...] = (slots[:, own_rows:] + gprecv[...]).T
 
@@ -507,9 +563,13 @@
         vm((LANES, LANES), F32),
         vm((rows_pad, vlocal), BF16),
         vm((2, nz, width // nz, HALF), BF16),
-        vm((2, nz - 1, width // nz, HALF), BF16),
+        vm((2, 2, width // nz, HALF), BF16),
+        vm((2, 2, width // nz, HALF // 2), BF16),
+        vm((2, 2, width // nz, HALF), BF16),
+        vm((2, 2, width // nz, HALF), BF16),
+        vm((2, 2, width // nz, HALF), BF16),
         vm((width // nz, rows_pad), F32),
-        vm((2, width, WCOLS), F32),
+        vm((3, width, WCOLS), F32),
         vm((chunks, width // 2, WCOLS), BF16),
         vm((chunks, width // 2, WCOLS), BF16),
         vm((chunks, nx, ny, share, WCOLS), BF16),
@@ -527,8 +587,8 @@
         dma((2,)),
         dma((2, nz - 1)),
         dma((2, nz - 1)),
-        dma((2, nz - 1)),
-        dma((2, nz - 1)),
+        dma((2, 8)),
+        dma((2, 8)),
         dma((chunks,)),
         dma((chunks,)),
         dma((chunks, nx + ny - 2)),

time: 63.8 us -> 58.9 us (0.923)
  Pallas kernels: 62.9 us -> 58 us
    pallas_call x1, Pallas kernels: 61.1 us -> 56.1 us  [body(): pl.pallas_call(functools.partial(kernel, grid), out_shape=(jax.ShapeDtype...]
where the time goes in v3:
time: 58.9 us; the launch traced here: 58.8 us
  Pallas kernels  58 us (98%)
  between operations  0.8 us (1%)
    pallas_call x1, Pallas kernels, body(): pl.pallas_call(functools.partial(kernel, grid), out_shape=(jax.ShapeDtype...  56.1 us
    pallas_call x1, Pallas kernels, body(): pl.pallas_call(handover, out_shape=tuple((jax.ShapeDtypeStruct(r.shape, r...  1.84 us

profile of v3, /device:TPU:1, one launch (start us, length us, event | category | flops | bytes accessed | tf_op | source)
XLA Modules:
  0.0 58.8 jit_solution(139928145873534676)
XLA Ops:
  0.6 56.1 %shard_map.121 = (f32[16,3840]{1,0:T(8,128)}, f32[64,192]{1,0:T(8,128)}, f32[256,64]{1,0:T(8,128)}) custom-call(bf16[192,512]{1,0:T(8,128)(2,1)} %enc_hbm.1, bf16[256,512]{1,0:T(8,128)(2,1)} %bitcast.10, bf16[512,3840]{1,0:T(8,128)(2,1)} %w_hbm.1, s32[1,192]{1,0:T(1,128)} %bitcast.14, s32[1,192]{1,0:T(1,128)} %bitcast.15, s32[5,192]{1,0:T(8,128)} %bitcast.11, ...), custom_call_target="tpu_custom_call" | custom-call | tf_op jit(solution)/shard_map/pallas_call | solution.py:600
  56.7 1.8 %shard_map.122 = (f32[16,3840]{1,0:T(8,128)}, f32[64,192]{1,0:T(8,128)}, f32[256,64]{1,0:T(8,128)}) custom-call(f32[16,3840]{1,0:T(8,128)} %get-tuple-element.9.refs_0_, f32[64,192]{1,0:T(8,128)} %get-tuple-element.10.refs_1_, f32[256,64]{1,0:T(8,128)} %get-tuple-element.11.refs_2_), custom_call_target="tpu_custom_call" | custom-call | tf_op jit(solution)/shard_map/pallas_call | solution.py:625

commit v4 on v3

--- a/solution.py
+++ b/solution.py
@@ -67,6 +67,7 @@
     srecv,
     scol,
     gbuf,
+    hsum,
     hsend,
     far,
     half_far,
@@ -77,7 +78,8 @@
     pbuf,
     csend,
     crecv,
-    wsum,
+    wleft,
+    wright,
     xr1,
     yst,
     yst32,
@@ -227,44 +229,42 @@
     loads[9].wait()
 
     stat_copies = []
-    for h in range(2):
+
+    def logits_cols(h, cols):
         r0 = h * HALF
         count = min(HALF, rows - r0)
-        mx[...] = jnp.full(mx.shape, -jnp.inf, F32)
-
-        def logits_step(c, carry, r0=r0, count=count):
-            cols = pl.ds(pl.multiple_of(c * LCOLS, LCOLS), LCOLS)
-            block = jnp.dot(actb[pl.ds(r0, count), :], w[:, cols], preferred_element_type=F32)
-            ebuf[pl.ds(r0, count), cols] = block
-            top = mx[pl.ds(0, count), :]
-            for t in range(LCOLS // LANES):
-                top = jnp.maximum(top, block[:, t * LANES : (t + 1) * LANES])
-            mx[pl.ds(0, count), :] = top
-            return carry
-
-        lax.fori_loop(0, vlocal // LCOLS, logits_step, 0)
-        peaks = jnp.max(mx[pl.ds(0, count), :], axis=1, keepdims=True)
-        mx[pl.ds(0, count), :] = jnp.broadcast_to(peaks, (count, LANES))
-
-        def exp_step(b, carry, r0=r0):
-            local = pl.ds(pl.multiple_of(b * EROWS, EROWS), EROWS)
-            at = pl.ds(pl.multiple_of(r0 + b * EROWS, EROWS), EROWS)
-            wide = mx[local, :]
-            total = jnp.zeros((EROWS, LANES), F32)
-            for t in range(vlocal // LANES):
-                cols = pl.ds(t * LANES, LANES)
-                e = jnp.exp(ebuf[at, cols] - wide)
-                ebuf[at, cols] = e
-                total = total + e
-            sums[local, :] = total
-            return carry
-
-        lax.fori_loop(0, count // EROWS, exp_step, 0)
+        block = jnp.dot(actb[pl.ds(r0, count), :], w[:, cols], preferred_element_type=F32)
+        ebuf[pl.ds(r0, count), cols] = block
+        top = mx[h, pl.ds(0, count), :]
+        for t in range(block.shape[1] // LANES):
+            top = jnp.maximum(top, block[:, t * LANES : (t + 1) * LANES])
+        mx[h, pl.ds(0, count), :] = top
+
+    def spread_peak(h):
+        count = min(HALF, rows - h * HALF)
+        peaks = jnp.max(mx[h, pl.ds(0, count), :], axis=1, keepdims=True)
+        mx[h, pl.ds(0, count), :] = jnp.broadcast_to(peaks, (count, LANES))
+
+    def exp_rows(h, first_row, count):
+        local = pl.ds(first_row, count)
+        at = pl.ds(h * HALF + first_row, count)
+        wide = mx[h, local, :]
+        total = jnp.zeros((count, LANES), F32)
+        for t in range(vlocal // LANES):
+            cols = pl.ds(t * LANES, LANES)
+            e = jnp.exp(ebuf[at, cols] - wide)
+            ebuf[at, cols] = e
+            total = total + e
+        sums[local, :] = total
+
+    def send_stats(h):
+        r0 = h * HALF
+        count = min(HALF, rows - r0)
         totals = jnp.sum(sums[pl.ds(0, count), :], axis=1, keepdims=True)
         group = iota((count, LANES), 0) // LANES
         lanes = iota((count, LANES), 1)
         stat[pl.ds(r0, count), :] = jnp.where(
-            lanes == group, mx[pl.ds(0, count), :], jnp.where(lanes == group + 4, totals, 0.0)
+            lanes == group, mx[h, pl.ds(0, count), :], jnp.where(lanes == group + 4, totals, 0.0)
         )
         packed = stat[pl.ds(r0, LANES), :]
         for b in range(1, 4):
@@ -279,11 +279,34 @@
             copies.append(cp)
         stat_copies.append(copies)
 
+    mx[...] = jnp.full(mx.shape, -jnp.inf, F32)
+
+    def logits_step(c, carry):
+        logits_cols(0, pl.ds(pl.multiple_of(c * LCOLS, LCOLS), LCOLS))
+        return carry
+
+    lax.fori_loop(0, vlocal // LCOLS, logits_step, 0)
+    spread_peak(0)
+    beside = 2
+    for c in range(vlocal // WCOLS):
+        logits_cols(1, pl.ds(c * WCOLS, WCOLS))
+        if c < beside:
+            exp_rows(0, c * (HALF // beside), HALF // beside)
+        if c == beside - 1:
+            send_stats(0)
+    spread_peak(1)
+
+    def exp_step(b, carry):
+        exp_rows(1, pl.multiple_of(b * EROWS, EROWS), EROWS)
+        return carry
+
+    lax.fori_loop(0, (rows - HALF) // EROWS, exp_step, 0)
+    send_stats(1)
+
     slice_rows = width // nz
 
-    def grad_half(h):
+    def grad_scale(h):
         r0 = h * HALF
-        count = min(HALF, rows - r0)
         for cp in stat_copies[h]:
             cp.wait()
         mine = ssend[h]
@@ -300,31 +323,28 @@
             at = pl.ds(r0 + b * LANES, LANES)
             frep[at, :] = jnp.broadcast_to(turned[:, b : b + 1], (LANES, LANES)) * coef[at, :]
 
-        def grad_step(b, carry):
-            at = pl.ds(pl.multiple_of(r0 + b * 32, 32), 32)
-            scale = frep[at, :]
-            label = labrep[at, :]
-            lcoef = lrep[at, :]
-            lanes = iota((32, LANES), 1)
-            for t in range(vlocal // LANES):
-                cols = pl.ds(t * LANES, LANES)
-                value = ebuf[at, cols] * scale - jnp.where(label - t * LANES == lanes, lcoef, 0.0)
-                if t == 0:
-                    value = value - bl0[at, :]
-                gbuf[at, cols] = value.astype(BF16)
-            return carry
-
-        lax.fori_loop(0, count // 32, grad_step, 0)
+    def grad_rows(first_row, count):
+        at = pl.ds(first_row, count)
+        scale = frep[at, :]
+        label = labrep[at, :]
+        lcoef = lrep[at, :]
+        lanes = iota((count, LANES), 1)
+        for t in range(vlocal // LANES):
+            cols = pl.ds(t * LANES, LANES)
+            value = ebuf[at, cols] * scale - jnp.where(label - t * LANES == lanes, lcoef, 0.0)
+            if t == 0:
+                value = value - bl0[at, :]
+            gbuf[at, cols] = value.astype(BF16)
 
     h_copies = {}
     relay_copies = {}
 
-    def hidden_half(h):
-        r0 = h * HALF
-        part = lax.dot_general(
-            w[...], gbuf[pl.ds(r0, HALF), :], (((1,), (1,)), ((), ())), preferred_element_type=F32
-        )
-        hsend[h] = part.astype(BF16).reshape(nz, slice_rows, HALF)
+    def hidden_cols(h, cols):
+        g = gbuf[pl.ds(h * HALF, HALF), cols]
+        return lax.dot_general(w[:, cols], g, (((1,), (1,)), ((), ())), preferred_element_type=F32)
+
+    def hidden_send(h):
+        hsend[h] = hsum[...].astype(BF16).reshape(nz, slice_rows, HALF)
         copies = []
         quarter = HALF // 2
         plan = [
@@ -392,8 +412,6 @@
         return slots, gp_copy
 
     chunks = vlocal // WCOLS
-    left = pl.ds(0, WCOLS // 2)
-    right = pl.ds(WCOLS // 2, WCOLS // 2)
     half_rows = width // 2
     c_copies, p1_copies, p2_copies = {}, {}, {}
 
@@ -412,11 +430,14 @@
         c_copies[c].wait()
         mine = pl.ds(pl.multiple_of(core * half_rows, half_rows), half_rows)
         both = pbuf[c % 3, mine, :] + crecv[c].astype(F32)
-        wsum[c] = both.astype(BF16).reshape(nx, ny, share, WCOLS)
+        both = both.astype(BF16).reshape(nx, ny, share, WCOLS)
+        wleft[c] = both[:, :, :, : WCOLS // 2]
+        for i in range(ny):
+            wright[c, i] = both[:, i, :, WCOLS // 2 :]
         copies = []
         for i in sorted(range(1, nx), key=lambda i: -min(i, nx - i)):
             cp = remote(
-                wsum.at[c, lax.rem(cx + i, nx), :, :, left],
+                wleft.at[c, lax.rem(cx + i, nx)],
                 xr1.at[c, i - 1],
                 p1_ssem.at[c, i - 1],
                 p1_rsem.at[c, i - 1],
@@ -426,7 +447,7 @@
             copies.append(cp)
         for i in sorted(range(1, ny), key=lambda i: -min(i, ny - i)):
             cp = remote(
-                wsum.at[c, :, lax.rem(cy + i, ny), :, right],
+                wright.at[c, lax.rem(cy + i, ny)],
                 yr1.at[c, i - 1],
                 p1_ssem.at[c, wx + i - 1],
                 p1_rsem.at[c, wx + i - 1],
@@ -439,12 +460,12 @@
     def weight_second(c):
         for cp in p1_copies[c]:
             cp.wait()
-        total = wsum[c, cx, :, :, left].astype(F32)
+        total = wleft[c, cx].astype(F32)
         for i in range(wx):
             total = total + xr1[c, i].astype(F32)
         yst32[c] = total
         yst[c] = total.astype(BF16)
-        total = wsum[c, :, cy, :, right].astype(F32)
+        total = wright[c, cy].astype(F32)
         for i in range(wy):
             total = total + yr1[c, i].astype(F32)
         xst32[c] = total
@@ -484,23 +505,43 @@
             total = total + xr2[c, i].astype(F32)
         gw_ref[:, pl.ds(c * WCOLS + WCOLS // 2, WCOLS // 2)] = total
 
-    grad_half(0)
-    hidden_half(0)
-    grad_half(1)
+    grad_scale(0)
+
+    def grad_step(b, carry):
+        grad_rows(pl.multiple_of(b * 64, 64), 64)
+        return carry
+
+    lax.fori_loop(0, HALF // 64, grad_step, 0)
+    alone = chunks * 2 // 5
+    spread = rows - HALF
+    part = -(-spread // (chunks - alone) // 16) * 16
+    for c in range(chunks):
+        if c == alone:
+            grad_scale(1)
+        value = hidden_cols(0, pl.ds(c * WCOLS, WCOLS))
+        hsum[...] = value if c == 0 else hsum[...] + value
+        if c >= alone:
+            done = (c - alone) * part
+            grad_rows(HALF + done, min(part, spread - done))
+    hidden_send(0)
     weight_chunk(0)
     weight_chunk(1)
+    hsum[...] = hidden_cols(1, pl.ds(0, vlocal))
+    hidden_send(1)
     weight_first(0)
-    hidden_half(1)
     relay_half(0)
     for c in range(2, chunks):
         weight_chunk(c)
-        weight_first(c - 1)
+        if c >= 3:
+            weight_first(c - 2)
+    weight_first(chunks - 2)
     weight_second(0)
     weight_first(chunks - 1)
     relay_half(1)
-    for c in range(1, chunks - 1):
+    for c in range(1, chunks - 2):
         weight_second(c)
     slots, gp_copy = hidden_finish()
+    weight_second(chunks - 2)
     weight_second(chunks - 1)
     for c in range(chunks):
         weight_last(c)
@@ -555,13 +596,14 @@
         vm((width, rows_pad), F32),
         vm((width, rows_pad), BF16),
         vm((frames * KEPT, vlocal), F32),
-        vm((HALF, LANES), F32),
+        vm((2, HALF, LANES), F32),
         vm((HALF, LANES), F32),
         vm((rows_pad, LANES), F32),
         vm((2, 8, LANES), F32),
         vm((2, nz - 1, 8, LANES), F32),
         vm((LANES, LANES), F32),
         vm((rows_pad, vlocal), BF16),
+        vm((width, HALF), F32),
         vm((2, nz, width // nz, HALF), BF16),
         vm((2, 2, width // nz, HALF), BF16),
         vm((2, 2, width // nz, HALF // 2), BF16),
@@ -572,7 +614,8 @@
         vm((3, width, WCOLS), F32),
         vm((chunks, width // 2, WCOLS), BF16),
         vm((chunks, width // 2, WCOLS), BF16),
-        vm((chunks, nx, ny, share, WCOLS), BF16),
+        vm((chunks, nx, ny, share, hw), BF16),
+        vm((chunks, ny, nx, share, hw), BF16),
         vm((chunks, nx - 1, ny, share, hw), BF16),
         vm((chunks, ny, share, hw), BF16),
         vm((chunks, ny, share, hw), F32),

time: 58.9 us -> 58.7 us (level); the launches traced: 58.8 us -> 57.9 us
  Pallas kernels: 58 us -> 57.1 us
    pallas_call x1, Pallas kernels: 56.1 us -> 55.2 us  [body(): pl.pallas_call(functools.partial(kernel, grid), out_shape=(jax.ShapeDtype...]
where the time goes in v4:
time: 58.7 us; the launch traced here: 57.9 us
  Pallas kernels  57.1 us (97%)
  between operations  0.8 us (1%)
    pallas_call x1, Pallas kernels, body(): pl.pallas_call(functools.partial(kernel, grid), out_shape=(jax.ShapeDtype...  55.2 us
    pallas_call x1, Pallas kernels, body(): pl.pallas_call(handover, out_shape=tuple((jax.ShapeDtypeStruct(r.shape, r...  1.84 us

profile of v4, /device:TPU:1, one launch (start us, length us, event | category | flops | bytes accessed | tf_op | source)
XLA Modules:
  0.0 57.9 jit_solution(11140398664461337536)
XLA Ops:
  0.6 55.2 %shard_map.121 = (f32[16,3840]{1,0:T(8,128)}, f32[64,192]{1,0:T(8,128)}, f32[256,64]{1,0:T(8,128)}) custom-call(bf16[192,512]{1,0:T(8,128)(2,1)} %enc_hbm.1, bf16[256,512]{1,0:T(8,128)(2,1)} %bitcast.10, bf16[512,3840]{1,0:T(8,128)(2,1)} %w_hbm.1, s32[1,192]{1,0:T(1,128)} %bitcast.14, s32[1,192]{1,0:T(1,128)} %bitcast.15, s32[5,192]{1,0:T(8,128)} %bitcast.11, ...), custom_call_target="tpu_custom_call" | custom-call | tf_op jit(solution)/shard_map/pallas_call | solution.py:643
  55.9 1.8 %shard_map.122 = (f32[16,3840]{1,0:T(8,128)}, f32[64,192]{1,0:T(8,128)}, f32[256,64]{1,0:T(8,128)}) custom-call(f32[16,3840]{1,0:T(8,128)} %get-tuple-element.9.refs_0_, f32[64,192]{1,0:T(8,128)} %get-tuple-element.10.refs_1_, f32[256,64]{1,0:T(8,128)} %get-tuple-element.11.refs_2_), custom_call_target="tpu_custom_call" | custom-call | tf_op jit(solution)/shard_map/pallas_call | solution.py:668
